TPU v7x, 32 devices: a whole 2x2x4 slice. The times are simulated.
32 devices in a mesh: grp: 2 (over y), page: 4 (over z), tp: 2 (over x), sub: 2 (over core).
Axes of the slice: x: 2, y: 2, z: 4, core: 2. Of those that a mesh axis runs over, the one named last changes fastest.
Arguments:
- tokens: bfloat16 [4096, 8192], P(('grp', 'page'), ('tp', 'sub')), parts along dimension 0, may hold values from -6 to 6
- base_value_weight: bfloat16 [8192, 1024], P(('tp', 'sub')), may hold values from -0.0625 to 0.0625
- adapter_down_weight: bfloat16 [16384, 1024], P(('grp', 'tp', 'sub'), 'page'), parts along dimension 0, may hold values from -0.0625 to 0.0625
- adapter_up_weight: bfloat16 [2048, 1024], P(('grp', 'page'), ('tp', 'sub')), parts along dimension 0, may hold values from -0.75 to 0.75
- row_adapter_index: int32 [4096], P(('grp', 'page')), parts along dimension 0, may hold values from 0 to 15, as said below
- adapter_storage_slot: int32 [32], P('grp'), parts along dimension 0, may hold values from 0 to 15, as said below
Outputs:
- values: bfloat16 [4096, 1024], P(('grp', 'page'), ('tp', 'sub')), parts along dimension 0
There are 2 independent parts, one for each index of `grp`. A program takes and returns all parts, laid end to end along the dimension named above; an argument that names none is the same for every part. Nothing has to cross between parts.
Inputs may be any that keep to these rules, and one draw needn't show every extreme that they name: `adapter_storage_slot`: adapter ids are the slots in some order: every value occurs once. `row_adapter_index`: of the 512 rows of one index of page, at most 256 have adapters whose slots lie in one page, and at most 384 have adapters whose slots lie in page j or page j + 2; in every draw one page receives exactly 256 rows and that pair of pages exactly 384 rows from every index of page.
All inputs are finite; a program needn't handle non-finite values.
Results may differ from a plain program's by a relative error of at most 0.0037.
Values may be sent and summed in bfloat16 or wider, within the bound.
A program may use at most 64 MiB of HBM per device.

v0:
```python
import jax
import jax.numpy as jnp
from jax import lax
from jax.sharding import PartitionSpec as P

ADAPTER_RANK = 64


adapter_scale = 0.5


def rank_within(labels, count):
    onehot = (labels[:, None] == jnp.arange(count, dtype=jnp.int32)[None, :]).astype(jnp.int32)
    before = jnp.cumsum(onehot, axis=0) - onehot
    return jnp.sum(before * onehot, axis=1)


def build_device_worker(down_cols, up_weight_rows):
    width = down_cols.shape[1]
    row_grouping = width // ADAPTER_RANK
    column_group = jnp.arange(width, dtype=jnp.int32) // ADAPTER_RANK

    def owner_work(pair):
        rows, marks = pair
        sources = marks.shape[0]
        count = marks.shape[1]
        feat = rows.shape[2]
        flat_rows = rows.reshape(sources * count, feat)
        owner_ids = marks.reshape(sources * count).astype(jnp.int32)
        select = owner_ids[:, None] == column_group[None, :]
        partial_all = jnp.dot(flat_rows, down_cols, preferred_element_type=jnp.float32)
        picked = (
            jnp.where(select, partial_all, 0.0)
            .reshape(sources * count, row_grouping, ADAPTER_RANK)
            .sum(axis=1)
        )
        shrink_rank = lax.psum(picked, ("tp", "sub")).astype(jnp.bfloat16)
        spread_rows = jnp.where(
            select, jnp.tile(shrink_rank, (1, row_grouping)), jnp.zeros((), jnp.bfloat16)
        )
        expand_rank = (
            jnp.dot(spread_rows, up_weight_rows, preferred_element_type=jnp.float32) * adapter_scale
        )
        return expand_rank.astype(jnp.bfloat16).reshape(sources, count, expand_rank.shape[1])

    return owner_work


def pack_boxes(tokens, flattened, marks, adapter_pages, slot_capacity):
    feat = tokens.shape[1]
    outbox = (
        jnp.zeros((adapter_pages * slot_capacity, feat), jnp.bfloat16).at[flattened].set(tokens)
    )
    labels = (
        jnp.full((adapter_pages * slot_capacity,), -1.0, jnp.bfloat16)
        .at[flattened]
        .set(marks.astype(jnp.bfloat16))
    )
    return (
        outbox.reshape(adapter_pages, slot_capacity, feat),
        labels.reshape(adapter_pages, slot_capacity),
    )


def body(
    tokens,
    base_value_weight,
    adapter_down_weight,
    adapter_up_weight,
    row_adapter_index,
    adapter_storage_slot,
):
    adapter_pages = lax.axis_size("page")
    row_dev = tokens.shape[0]
    slot_capacity = min(4 * row_dev // adapter_pages, row_dev // 2)
    row_grouping = adapter_down_weight.shape[1] // ADAPTER_RANK
    hits = (
        row_adapter_index[:, None]
        == jnp.arange(adapter_storage_slot.shape[0], dtype=jnp.int32)[None, :]
    )
    storage_position = jnp.sum(jnp.where(hits, adapter_storage_slot[None, :], 0), axis=1)
    target = storage_position // row_grouping
    within = storage_position % row_grouping
    position = rank_within(target, adapter_pages)
    flattened = target * slot_capacity + position
    outbox, labels = pack_boxes(tokens, flattened, within, adapter_pages, slot_capacity)
    device_worker = build_device_worker(adapter_down_weight, adapter_up_weight)
    finished = device_worker(
        (
            lax.all_to_all(outbox, "page", split_axis=0, concat_axis=0, tiled=True),
            lax.all_to_all(labels, "page", split_axis=0, concat_axis=0, tiled=True),
        )
    )
    returned_output = lax.all_to_all(finished, "page", split_axis=0, concat_axis=0, tiled=True)
    adapter_row_output = returned_output.reshape(
        adapter_pages * slot_capacity, returned_output.shape[2]
    )[flattened]
    partial_base = jnp.dot(tokens, base_value_weight, preferred_element_type=jnp.float32)
    base_output_share = lax.psum_scatter(
        partial_base, ("tp", "sub"), scatter_dimension=1, tiled=True
    )
    return (base_output_share + adapter_row_output.astype(jnp.float32)).astype(jnp.bfloat16)


def solution(mesh):
    return jax.shard_map(
        body,
        mesh=mesh,
        in_specs=(
            P(("grp", "page"), ("tp", "sub")),
            P(("tp", "sub"), None),
            P(("grp", "tp", "sub"), "page"),
            P(("grp", "page"), ("tp", "sub")),
            P(("grp", "page")),
            P("grp"),
        ),
        out_specs=P(("grp", "page"), ("tp", "sub")),
        check_vma=False,
    )
```

profile of v0, /device:TPU:0, one launch (start us, length us, event | category | flops | bytes accessed | tf_op | source)
XLA Modules:
  0.0 174.1 jit_solution(9204589419389952313)
XLA Ops:
  6.5 0.0 copy-start
  6.5 0.9 select_reduce_fusion
  7.4 1.2 reduce-window.6
  8.7 0.2 slice_reduce_fusion
  8.9 0.2 reduce-window.9
  9.1 0.1 add_bitcast_fusion
  9.2 3.8 %scatter_custom_fusion = bf16[1024]{0:T(1024)(128)(2,1)S(1)} fusion(s32[512]{0:T(512)S(1)} %bitcast.55, bf16[512]{0:T(512)(128)(2,1)S(1)} %get-tuple-element.5, bf16[]{:T(256)} %constant.48.clone.1), kind=kCustom, calls=%fused_computation.52 | custom fusion | bytes 2050 | tf_op jit(solution)/shard_map/scatter | solution.py:57
  13.0 0.5 broadcast.184
  13.5 0.7 reduce.2
  14.2 0.6 reshape.170
  14.8 6.3 %all-to-all-start = ((bf16[4,2,128]{2,1,0:T(2,128)(2,1)}), bf16[4,2,128]{2,1,0:T(2,128)(2,1)S(1)}, u32[]{:S(2)}, u32[]{:S(2)}) async-start(bf16[4,2,128]{2,1,0:T(2,128)(2,1)} %reshape.170), calls=%async_computation.1 | async-start | bytes 4096 | tf_op jit(solution)/shard_map/all_to_all | solution.py:91
  21.1 7.3 %scatter_custom_fusion.1 = bf16[1024,2048]{1,0:T(8,128)(2,1)} fusion(s32[512]{0:T(512)S(1)} %bitcast.56, bf16[512,2048]{1,0:T(8,128)(2,1)} %param.6, bf16[]{:T(256)} %constant.59.clone.1), kind=kCustom, calls=%fused_computation.3 | custom fusion | bytes 4194816 | tf_op jit(solution)/shard_map/scatter | solution.py:52
  28.3 0.0 all-to-all-done
  28.3 0.0 copy-start.1
  28.3 5.2 %all-to-all-start.1 = ((bf16[4,256,2048]{2,1,0:T(8,128)(2,1)}), bf16[4,256,2048]{2,1,0:T(8,128)(2,1)}, u32[]{:S(2)}, u32[]{:S(2)}) async-start(bf16[4,256,2048]{2,1,0:T(8,128)(2,1)} %bitcast.50), calls=%async_computation.2 | async-start | bytes 8388608 | tf_op jit(solution)/shard_map/all_to_all | solution.py:90
  33.6 0.0 reduce-scatter.2.cloned.1.call-start
  33.6 0.0 copy-done.1
  33.6 5.9 %fusion.18 = f32[512,1024]{1,0:T(8,128)} fusion(bf16[512,2048]{1,0:T(8,128)(2,1)S(1)} %copy-done.1, bf16[2048,1024]{1,0:T(8,128)(2,1)} %param.7), kind=kOutput, calls=%fused_computation.55 | convolution fusion | flops 2147483648 | bytes 8388608 | tf_op jit(solution)/shard_map/dot_general | solution.py:98
  39.5 0.0 reduce-scatter.2.cloned.1.call-update
  39.6 87.0 %all-to-all-done.1 = bf16[4,256,2048]{2,1,0:T(8,128)(2,1)} async-done(((bf16[4,256,2048]{2,1,0:T(8,128)(2,1)}), bf16[4,256,2048]{2,1,0:T(8,128)(2,1)}, u32[]{:S(2)}, u32[]{:S(2)}) %all-to-all-start.1) | async-done | bytes 4194336 | tf_op jit(solution)/shard_map/all_to_all | solution.py:90
  126.5 0.0 copy-done
  126.5 3.5 %compare_select_fusion.1 = f32[1024,256]{0,1:T(8,128)S(1)} fusion(bf16[1024,2048]{1,0:T(8,128)(2,1)} %bitcast.7, bf16[2048,256]{1,0:T(8,128)(2,1)S(1)} %copy-done, s32[1024]{0:T(1024)S(1)} %bitcast.60, s32[256]{0:T(256)S(1)} %and_select_fusion.1), kind=kOutput, calls=%fused_computation.7 | convolution fusion | flops 1074266112 | bytes 6296576 | tf_op jit(solution)/shard_map/dot_general | solution.py:31
  130.1 0.1 reduce_sum.38
  130.2 13.1 %all-reduce.1 = bf16[1024,64]{0,1:T(8,128)(2,1)S(1)} all-reduce(f32[1024,64]{0,1:T(8,128)S(1)} %reduce_sum.38), channel_id=1, replica_groups=mesh['grp'=2,'page'=4,'tp'=2,'sub'=2] {'tp','sub'}, use_global_device_ids=true, to_apply=%region_8.9 | all-reduce | flops 65536 | bytes 393216 | tf_op jit(solution)/shard_map/psum | solution.py:37
  143.2 0.1 tile.4
  143.3 0.0 copy-done.2
  143.3 1.2 fusion.2
  144.5 3.5 %all-to-all-start.2 = ((bf16[4,256,256]{2,1,0:T(8,128)(2,1)}), bf16[4,256,256]{2,1,0:T(8,128)(2,1)S(1)}, u32[]{:S(2)}, u32[]{:S(2)}) async-start(bf16[4,256,256]{2,1,0:T(8,128)(2,1)} %bitcast.10), calls=%async_computation.3 | async-start | bytes 1048576 | tf_op jit(solution)/shard_map/all_to_all | solution.py:94
  148.0 15.4 %all-to-all-done.2 = bf16[4,256,256]{2,1,0:T(8,128)(2,1)S(1)} async-done(((bf16[4,256,256]{2,1,0:T(8,128)(2,1)}), bf16[4,256,256]{2,1,0:T(8,128)(2,1)S(1)}, u32[]{:S(2)}, u32[]{:S(2)}) %all-to-all-start.2) | async-done | bytes 524320 | tf_op jit(solution)/shard_map/all_to_all | solution.py:94
  163.5 1.9 %gather_fusion = bf16[512,256]{1,0:T(8,128)(2,1)S(1)} fusion(bf16[1024,256]{1,0:T(8,128)(2,1)S(1)} %bitcast.51, s32[1024]{0:T(1024)S(1)} %pad_clamp_fusion), kind=kCustom, calls=%fused_computation | custom fusion | bytes 526336 | tf_op jit(solution)/shard_map/gather | solution.py:95
  165.4 0.0 reduce-scatter.2.cloned.1.call-done
  165.4 1.8 %add_convert_fusion = bf16[512,256]{1,0:T(8,128)(2,1)} fusion(f32[512,256]{1,0:T(8,128)} %reduce-scatter.2.cloned.1.call-done, bf16[512,256]{1,0:T(8,128)(2,1)S(1)} %gather_fusion), kind=kLoop, calls=%fused_computation.9 | loop fusion | flops 393216 | bytes 1048576 | tf_op jit(solution)/shard_map/convert_element_type | solution.py:102
  (11 shorter events, 0.1 us)
Async XLA Ops:
  6.5 120.0 %copy-start = (bf16[2048,256]{1,0:T(8,128)(2,1)S(1)}, bf16[2048,256]{1,0:T(8,128)(2,1)}, u32[]{:S(2)}) copy-start(bf16[2048,256]{1,0:T(8,128)(2,1)} %param.8) | copy-start | bytes 3145732
  14.8 13.6 %all-to-all-start = ((bf16[4,2,128]{2,1,0:T(2,128)(2,1)}), bf16[4,2,128]{2,1,0:T(2,128)(2,1)S(1)}, u32[]{:S(2)}, u32[]{:S(2)}) async-start(bf16[4,2,128]{2,1,0:T(2,128)(2,1)} %reshape.170), calls=%async_computation.1 | async-start | bytes 4096 | tf_op jit(solution)/shard_map/all_to_all | solution.py:91
  28.3 5.2 %copy-start.1 = (bf16[512,2048]{1,0:T(8,128)(2,1)S(1)}, bf16[512,2048]{1,0:T(8,128)(2,1)}, u32[]{:S(2)}) copy-start(bf16[512,2048]{1,0:T(8,128)(2,1)} %param.6) | copy-start | bytes 6291460
  28.3 98.2 %all-to-all-start.1 = ((bf16[4,256,2048]{2,1,0:T(8,128)(2,1)}), bf16[4,256,2048]{2,1,0:T(8,128)(2,1)}, u32[]{:S(2)}, u32[]{:S(2)}) async-start(bf16[4,256,2048]{2,1,0:T(8,128)(2,1)} %bitcast.50), calls=%async_computation.2 | async-start | bytes 8388608 | tf_op jit(solution)/shard_map/all_to_all | solution.py:90
  33.6 131.9 %reduce-scatter.2.cloned.1.call-start = ((), (), s32[]{:S(2)}) async-start(), calls=%async_computation.4 | async-start | bytes 2621440 | tf_op jit(solution)/shard_map/reduce_scatter | solution.py:99
  126.5 16.7 %copy-start.2 = (bf16[256,256]{1,0:T(8,128)(2,1)S(1)}, bf16[256,256]{1,0:T(8,128)(2,1)}, u32[]{:S(2)}) copy-start(bf16[256,256]{1,0:T(8,128)(2,1)} %param.9) | copy-start | bytes 393220
  144.5 18.9 %all-to-all-start.2 = ((bf16[4,256,256]{2,1,0:T(8,128)(2,1)}), bf16[4,256,256]{2,1,0:T(8,128)(2,1)S(1)}, u32[]{:S(2)}, u32[]{:S(2)}) async-start(bf16[4,256,256]{2,1,0:T(8,128)(2,1)} %bitcast.10), calls=%async_computation.3 | async-start | bytes 1048576 | tf_op jit(solution)/shard_map/all_to_all | solution.py:94
Sparse Core Ops, SparseCore 0:
  39.7 32.8 reduce-scatter.1
where the time goes:
time: 175 us; the launch traced here: 174 us
  waiting for transfers between devices  102 us (58%)
  starting transfers between devices  15 us (9%)
  local copies, waits for them, and re-layouts  14.4 us (8%)
  between operations  13.5 us (8%)
  blocking collectives  13.1 us (7%)
  matrix products  10.7 us (6%)
  other arithmetic  5 us (3%)
    all_to_all x1, waiting for transfers between devices, body(): lax.all_to_all(outbox, 'page', split_axis=0, concat_axis=0, tiled=True)  87 us
    all_to_all x1, waiting for transfers between devices, body(): lax.all_to_all(finished, 'page', split_axis=0, concat_axis=0, tiled=True)  15.4 us
    psum x1, blocking collectives, owner_work(): shrink_rank = lax.psum(picked, ('tp', 'sub')).astype(jnp.bfloat16)  13.1 us
    scatter x1, local copies, waits for them, and re-layouts, pack_boxes(): jnp.zeros((adapter_pages * slot_capacity, feat), jnp.bfloat16).at[flattened]  7.25 us
    all_to_all x1, starting transfers between devices, body(): lax.all_to_all(labels, 'page', split_axis=0, concat_axis=0, tiled=True)  6.32 us
    dot_general x1, matrix products, body(): jnp.dot(tokens, base_value_weight, preferred_element_type=jnp.float32)  5.93 us
    all_to_all x1, starting transfers between devices, body(): lax.all_to_all(outbox, 'page', split_axis=0, concat_axis=0, tiled=True)  5.22 us
    scatter x1, local copies, waits for them, and re-layouts, pack_boxes(): labels = jnp.full((adapter_pages * slot_capacity,), -1.0, jnp.bfloat16).a...  3.77 us
  transfers between devices with their start and end apart: 4, of which 2 were waited for; matrix products, arithmetic and copies ran while one was open for 12% of the time, Pallas kernels for 0%

commit v1 on v0

--- a/solution.py
+++ b/solution.py
@@ -1,6 +1,10 @@
+import functools
+
 import jax
 import jax.numpy as jnp
 from jax import lax
+from jax.experimental import pallas as pl
+from jax.experimental.pallas import tpu as pltpu
 from jax.sharding import PartitionSpec as P
 
 ADAPTER_RANK = 64
@@ -62,7 +66,7 @@
     )
 
 
-def body(
+def exchange_rows_body(
     tokens,
     base_value_weight,
     adapter_down_weight,
@@ -102,9 +106,302 @@
     return (base_output_share + adapter_row_output.astype(jnp.float32)).astype(jnp.bfloat16)
 
 
+MESH_ID = pl.DeviceIdType.MESH
+CHUNKS = 2
+
+
+def page_in_turn(z, turn, n):
+    if turn == 0:
+        return z
+    nearer = jnp.minimum(z, n - 1 - z)
+    step = -((turn + 1) // 2) if turn % 2 else turn // 2
+    beyond = jnp.where(z < n - 1 - z, z + (turn - nearer), z - (turn - nearer))
+    return jnp.where(turn <= 2 * nearer, z + step, beyond)
+
+
+def gather_kernel(
+    n,
+    adapters,
+    tokens_hbm,
+    base_hbm,
+    down_hbm,
+    up_hbm,
+    index_ref,
+    slot_ref,
+    out_ref,
+    tok,
+    basew,
+    down_all,
+    up_all,
+    part,
+    picked,
+    near_base,
+    far_base,
+    shrink_send,
+    near_shrink,
+    far_send,
+    far_shrink,
+    load_sem,
+    right_sem,
+    left_sem,
+    recv_sem,
+    sum_send_sem,
+    sum_recv_sem,
+):
+    z, t, s = lax.axis_index("page"), lax.axis_index("tp"), lax.axis_index("sub")
+    rows, depth = tok.shape
+    rank = ADAPTER_RANK
+    group = down_all.shape[2] // rank
+    piece = depth // CHUNKS
+
+    loads = [
+        pltpu.make_async_copy(down_hbm, down_all.at[z], load_sem.at[0]),
+        pltpu.make_async_copy(up_hbm, up_all.at[z], load_sem.at[1]),
+        pltpu.make_async_copy(tokens_hbm, tok, load_sem.at[2]),
+        pltpu.make_async_copy(base_hbm, basew, load_sem.at[3]),
+    ]
+    for load in loads:
+        load.start()
+
+    barrier = pltpu.get_barrier_semaphore()
+    pl.semaphore_signal(barrier, inc=1, device_id={"tp": 1 - t}, device_id_type=MESH_ID)
+    pl.semaphore_signal(barrier, inc=1, device_id={"sub": 1 - s}, device_id_type=MESH_ID)
+
+    @pl.when(z > 0)
+    def _():
+        pl.semaphore_signal(barrier, inc=1, device_id={"page": z - 1}, device_id_type=MESH_ID)
+
+    @pl.when(z < n - 1)
+    def _():
+        pl.semaphore_signal(barrier, inc=1, device_id={"page": z + 1}, device_id_type=MESH_ID)
+
+    pl.semaphore_wait(barrier, 2 + (z > 0).astype(jnp.int32) + (z < n - 1).astype(jnp.int32))
+
+    def hop(page, chunk, to, sems):
+        if chunk < CHUNKS:
+            ref = down_all.at[page, pl.ds(chunk * piece, piece), :]
+        else:
+            ref = up_all.at[page]
+        return pltpu.make_async_remote_copy(
+            src_ref=ref,
+            dst_ref=ref,
+            send_sem=sems.at[page, chunk],
+            recv_sem=recv_sem.at[page, chunk],
+            device_id={"page": to},
+            device_id_type=MESH_ID,
+        )
+
+    def send_on(page, chunk):
+        @pl.when((page <= z) & (z < n - 1))
+        def _():
+            hop(page, chunk, z + 1, right_sem).start()
+
+        @pl.when((page >= z) & (z > 0))
+        def _():
+            hop(page, chunk, z - 1, left_sem).start()
+
+    loads[0].wait()
+    for chunk in range(CHUNKS):
+        send_on(z, chunk)
+    loads[1].wait()
+    send_on(z, CHUNKS)
+
+    slot_row = jnp.zeros(index_ref.shape, jnp.float32)
+    for a in range(adapters):
+        slot_row = jnp.where(index_ref[...] == a, slot_ref[a].astype(jnp.float32), slot_row)
+    slot = jnp.transpose(jnp.broadcast_to(slot_row, (128, rows)))
+    lane = lax.broadcasted_iota(jnp.int32, (rows, 128), 1)
+    half = (lane // rank).astype(jnp.float32)
+    loads[2].wait()
+    loads[3].wait()
+    blocks, width = part.shape[0], part.shape[2]
+
+    @pl.loop(0, blocks)
+    def _(b):
+        columns = pl.ds(pl.multiple_of(b * width, width), width)
+        part[b] = jnp.dot(tok[...], basew[:, columns], preferred_element_type=jnp.float32)
+
+    def to_sibling(k):
+        return pltpu.make_async_remote_copy(
+            src_ref=part.at[2 * k + 1 - s],
+            dst_ref=near_base.at[k],
+            send_sem=sum_send_sem.at[k],
+            recv_sem=sum_recv_sem.at[k],
+            device_id={"sub": 1 - s},
+            device_id_type=MESH_ID,
+        )
+
+    base_far = pltpu.make_async_remote_copy(
+        src_ref=part.at[2 * (1 - t) + s],
+        dst_ref=far_base,
+        send_sem=sum_send_sem.at[2],
+        recv_sem=sum_recv_sem.at[2],
+        device_id={"tp": 1 - t},
+        device_id_type=MESH_ID,
+    )
+    for k in range(2):
+        to_sibling(k).start()
+
+    def pick(page, product):
+        first = (page * group).astype(jnp.float32) + half
+        total = jnp.zeros((rows, 128), jnp.float32)
+        for g in range(group * rank // 128):
+            hit = slot == first + float(g * (128 // rank))
+            total += jnp.where(hit, product[:, g * 128 : g * 128 + 128], 0.0)
+        return total
+
+    for turn in range(n):
+        page = page_in_turn(z, turn, n)
+        for chunk in range(CHUNKS):
+            if turn:
+                hop(page, chunk, z, left_sem).wait_recv()
+                send_on(page, chunk)
+            span = pl.ds(chunk * piece, piece)
+            product = jnp.dot(
+                tok[:, chunk * piece : chunk * piece + piece],
+                down_all[page, span, :],
+                preferred_element_type=jnp.float32,
+            )
+            if turn == 0 and chunk == 0:
+                picked[...] = pick(page, product)
+            else:
+                picked[...] += pick(page, product)
+        if turn:
+            hop(page, CHUNKS, z, left_sem).wait_recv()
+            send_on(page, CHUNKS)
+        if turn == 0:
+            for k in range(2):
+                to_sibling(k).wait_recv()
+            part[2 * (1 - t) + s] += near_base[1 - t]
+            base_far.start()
+
+    folded = picked[...] + pltpu.roll(picked[...], rank, 1)
+    low = lane[: rows // 2] < rank
+    shrink_send[...] = jnp.where(low, folded[: rows // 2], folded[rows // 2 :])
+    near = pltpu.make_async_remote_copy(
+        src_ref=shrink_send,
+        dst_ref=near_shrink,
+        send_sem=sum_send_sem.at[3],
+        recv_sem=sum_recv_sem.at[3],
+        device_id={"sub": 1 - s},
+        device_id_type=MESH_ID,
+    )
+    near.start()
+    near.wait_recv()
+    far_send[...] = shrink_send[...] + near_shrink[...]
+    far = pltpu.make_async_remote_copy(
+        src_ref=far_send,
+        dst_ref=far_shrink,
+        send_sem=sum_send_sem.at[4],
+        recv_sem=sum_recv_sem.at[4],
+        device_id={"tp": 1 - t},
+        device_id_type=MESH_ID,
+    )
+    far.start()
+    base_far.wait_recv()
+    part[2 * t + s] += near_base[t] + far_base[...]
+    far.wait_recv()
+    both = far_send[...] + far_shrink[...]
+    both = both.astype(jnp.bfloat16).astype(jnp.float32)
+    turned = pltpu.roll(both, rank, 1)
+    shrink = jnp.concatenate(
+        [jnp.where(low, both, turned), jnp.where(low, turned, both)], axis=0
+    )
+    spread = jnp.concatenate(
+        [
+            jnp.where(slot == half + float(b * (128 // rank)), shrink, 0.0).astype(jnp.bfloat16)
+            for b in range(n * group * rank // 128)
+        ],
+        axis=1,
+    )
+    expand = jnp.dot(
+        spread,
+        up_all[...].reshape(n * group * rank, up_all.shape[2]),
+        preferred_element_type=jnp.float32,
+    )
+    lora = (expand * adapter_scale).astype(jnp.bfloat16).astype(jnp.float32)
+    out_ref[...] = (part[2 * t + s] + lora).astype(jnp.bfloat16)
+
+    for k in range(2):
+        to_sibling(k).wait_send()
+    base_far.wait_send()
+    near.wait_send()
+    far.wait_send()
+    for turn in range(n):
+        page = page_in_turn(z, turn, n)
+        for chunk in range(CHUNKS + 1):
+
+            @pl.when((page <= z) & (z < n - 1))
+            def _():
+                hop(page, chunk, z + 1, right_sem).wait_send()
+
+            @pl.when((page >= z) & (z > 0))
+            def _():
+                hop(page, chunk, z - 1, left_sem).wait_send()
+
+
+def gather_weights_body(
+    tokens,
+    base_value_weight,
+    adapter_down_weight,
+    adapter_up_weight,
+    row_adapter_index,
+    adapter_storage_slot,
+):
+    n = lax.axis_size("page")
+    rows, depth = tokens.shape
+    width = adapter_down_weight.shape[1]
+    share = adapter_up_weight.shape[1]
+    blocks = base_value_weight.shape[1] // share
+    adapters = adapter_storage_slot.shape[0]
+    f32, bf16 = jnp.float32, jnp.bfloat16
+    return pl.pallas_call(
+        functools.partial(gather_kernel, n, adapters),
+        out_shape=jax.ShapeDtypeStruct((rows, share), bf16),
+        in_specs=[pl.BlockSpec(memory_space=pl.ANY)] * 4
+        + [
+            pl.BlockSpec(memory_space=pltpu.VMEM),
+            pl.BlockSpec(memory_space=pltpu.SMEM),
+        ],
+        out_specs=pl.BlockSpec(memory_space=pltpu.VMEM),
+        scratch_shapes=[
+            pltpu.VMEM((rows, depth), bf16),
+            pltpu.VMEM(base_value_weight.shape, bf16),
+            pltpu.VMEM((n, depth, width), bf16),
+            pltpu.VMEM((n, width, share), bf16),
+            pltpu.VMEM((blocks, rows, share), f32),
+            pltpu.VMEM((rows, 128), f32),
+            pltpu.VMEM((2, rows, share), f32),
+            pltpu.VMEM((rows, share), f32),
+            pltpu.VMEM((rows // 2, 128), f32),
+            pltpu.VMEM((rows // 2, 128), f32),
+            pltpu.VMEM((rows // 2, 128), f32),
+            pltpu.VMEM((rows // 2, 128), f32),
+            pltpu.SemaphoreType.DMA((4,)),
+            pltpu.SemaphoreType.DMA((n, CHUNKS + 1)),
+            pltpu.SemaphoreType.DMA((n, CHUNKS + 1)),
+            pltpu.SemaphoreType.DMA((n, CHUNKS + 1)),
+            pltpu.SemaphoreType.DMA((5,)),
+            pltpu.SemaphoreType.DMA((5,)),
+        ],
+        compiler_params=pltpu.CompilerParams(
+            collective_id=0, has_side_effects=True, vmem_limit_bytes=48 * 1024 * 1024
+        ),
+    )(
+        tokens,
+        base_value_weight,
+        adapter_down_weight,
+        adapter_up_weight,
+        row_adapter_index.reshape(1, rows),
+        adapter_storage_slot,
+    )
+
+
 def solution(mesh):
+    sizes = mesh.shape
+    gathers = sizes["page"] <= 4 and sizes["tp"] == 2 and sizes["sub"] == 2
     return jax.shard_map(
-        body,
+        gather_weights_body if gathers else exchange_rows_body,
         mesh=mesh,
         in_specs=(
             P(("grp", "page"), ("tp", "sub")),

time: 175 us -> 94.7 us (0.54)
  waiting for transfers between devices: 102 us -> 0 us
  Pallas kernels: 0 us -> 88.6 us
  starting transfers between devices: 15 us -> 0 us
  between operations: 13.5 us -> 0.01 us
  blocking collectives: 13.1 us -> 0 us
  matrix products: 10.7 us -> 0 us
  local copies, waits for them, and re-layouts: 14.4 us -> 5.76 us
  other arithmetic: 5 us -> 0 us
    all_to_all x3 -> x0, waiting for transfers between devices: 102 us -> none  [the longest x1 87 us: body(): lax.all_to_all(outbox, 'page', split_axis=0, concat_axis=0, tiled=True)]
    pallas_call x0 -> x1, Pallas kernels: none -> 88.6 us  [gather_weights_body(): pl.pallas_call(functools.partial(gather_kernel, n, adapters), out_shape=j...]
    all_to_all x3 -> x0, starting transfers between devices: 15 us -> none  [the longest x1 6.32 us: body(): lax.all_to_all(labels, 'page', split_axis=0, concat_axis=0, tiled=True)]
    psum x1 -> x0, blocking collectives: 13.1 us -> none  [owner_work(): shrink_rank = lax.psum(picked, ('tp', 'sub')).astype(jnp.bfloat16)]
    scatter x2 -> x0, local copies, waits for them, and re-layouts: 11 us -> none  [the longest x1 7.25 us: pack_boxes(): jnp.zeros((adapter_pages * slot_capacity, feat), jnp.bfloat16).at[flattened]]
    dot_general x3 -> x0, matrix products: 10.7 us -> none  [the longest x1 5.93 us: body(): jnp.dot(tokens, base_value_weight, preferred_element_type=jnp.float32)]
    unnamed x8 -> x11, local copies, waits for them, and re-layouts: 0.61 us -> 5.76 us
    gather x1 -> x0, local copies, waits for them, and re-layouts: 1.95 us -> none  [body(): returned_output.reshape(adapter_pages * slot_capacity, returned_output.sh...]
  transfers between devices with their start and end apart: 4 -> 0, of which waited for: 2 -> 0; matrix products, arithmetic and copies ran while one was open for 12% -> 0% of each run, Pallas kernels for 0% -> 0%
where the time goes in v1:
time: 94.7 us; the launch traced here: 94.4 us
  Pallas kernels  88.6 us (94%)
  local copies, waits for them, and re-layouts  5.76 us (6%)
    pallas_call x1, Pallas kernels, gather_weights_body(): pl.pallas_call(functools.partial(gather_kernel, n, adapters), out_shape=j...  88.6 us
    unnamed x11, local copies, waits for them, and re-layouts  5.76 us

profile of v1, /device:TPU:0, one launch (start us, length us, event | category | flops | bytes accessed | tf_op | source)
XLA Modules:
  0.0 94.4 jit_solution(13490886611270502440)
XLA Ops:
  0.0 0.0 copy-start
  0.0 1.6 %copy-done = bf16[512,2048]{1,0:T(8,128)(2,1)S(1)} copy-done((bf16[512,2048]{1,0:T(8,128)(2,1)S(1)}, bf16[512,2048]{1,0:T(8,128)(2,1)}, u32[]{:S(2)}) %copy-start) | copy-done | bytes 2097176
  1.6 0.0 copy-start.1
  1.6 1.2 %copy-done.1 = bf16[2048,256]{1,0:T(8,128)(2,1)S(1)} copy-done((bf16[2048,256]{1,0:T(8,128)(2,1)S(1)}, bf16[2048,256]{1,0:T(8,128)(2,1)}, u32[]{:S(2)}) %copy-start.1) | copy-done | bytes 1048600
  2.8 0.0 copy-start.2
  2.8 0.9 copy-done.2
  3.7 0.0 copy-start.3
  3.7 0.7 copy-done.3
  4.4 0.0 copy-start.4
  4.4 0.7 copy-done.4
  5.1 88.6 %shard_map.64 = bf16[512,256]{1,0:T(8,128)(2,1)S(1)} custom-call(bf16[512,2048]{1,0:T(8,128)(2,1)S(1)} %copy-done, bf16[2048,1024]{1,0:T(8,128)(2,1)} %base_hbm.1, bf16[2048,256]{1,0:T(8,128)(2,1)S(1)} %copy-done.1, bf16[256,256]{1,0:T(8,128)(2,1)S(1)} %copy-done.2, s32[1,512]{1,0:T(1,128)S(1)} %bitcast.1, s32[16]{0:T(128)S(1)} %copy-done.4), custom_call_target="tpu_custom_call" | custom-call | tf_op jit(solution)/shard_map/pallas_call | solution.py:358
  93.7 0.7 copy.8
Async XLA Ops:
  0.0 1.6 %copy-start = (bf16[512,2048]{1,0:T(8,128)(2,1)S(1)}, bf16[512,2048]{1,0:T(8,128)(2,1)}, u32[]{:S(2)}) copy-start(bf16[512,2048]{1,0:T(8,128)(2,1)} %tokens_hbm.1) | copy-start | bytes 6291460
  1.6 1.2 %copy-start.1 = (bf16[2048,256]{1,0:T(8,128)(2,1)S(1)}, bf16[2048,256]{1,0:T(8,128)(2,1)}, u32[]{:S(2)}) copy-start(bf16[2048,256]{1,0:T(8,128)(2,1)} %down_hbm.1) | copy-start | bytes 3145732
  2.8 0.9 copy-start.2
  3.7 0.7 copy-start.3
  4.4 0.7 copy-start.4

commit v2 on v1

--- a/solution.py
+++ b/solution.py
@@ -126,13 +126,20 @@
     base_hbm,
     down_hbm,
     up_hbm,
+    index_hbm,
+    slot_hbm,
+    out_ref,
     index_ref,
     slot_ref,
-    out_ref,
     tok,
     basew,
     down_all,
     up_all,
+    pack,
+    pack_slot,
+    place,
+    pack_send,
+    pack_back,
     part,
     picked,
     near_base,
@@ -145,6 +152,8 @@
     right_sem,
     left_sem,
     recv_sem,
+    pack_send_sem,
+    pack_recv_sem,
     sum_send_sem,
     sum_recv_sem,
 ):
@@ -159,6 +168,8 @@
         pltpu.make_async_copy(up_hbm, up_all.at[z], load_sem.at[1]),
         pltpu.make_async_copy(tokens_hbm, tok, load_sem.at[2]),
         pltpu.make_async_copy(base_hbm, basew, load_sem.at[3]),
+        pltpu.make_async_copy(index_hbm, index_ref, load_sem.at[4]),
+        pltpu.make_async_copy(slot_hbm, slot_ref, load_sem.at[5]),
     ]
     for load in loads:
         load.start()
@@ -177,13 +188,20 @@
 
     pl.semaphore_wait(barrier, 2 + (z > 0).astype(jnp.int32) + (z < n - 1).astype(jnp.int32))
 
-    def hop(page, chunk, to, sems):
+    end = (z == 0) | (z == n - 1)
+    helped = jnp.where(z == 1, 0, n - 1)
+    helper = jnp.where(z == 0, 1, n - 2)
+    opposite = n - 1 - z
+
+    def hop(page, chunk, to, sems, own=False):
         if chunk < CHUNKS:
             ref = down_all.at[page, pl.ds(chunk * piece, piece), :]
+            src = down_hbm.at[pl.ds(chunk * piece, piece), :] if own else ref
         else:
             ref = up_all.at[page]
+            src = up_hbm if own else ref
         return pltpu.make_async_remote_copy(
-            src_ref=ref,
+            src_ref=src,
             dst_ref=ref,
             send_sem=sems.at[page, chunk],
             recv_sem=recv_sem.at[page, chunk],
@@ -191,21 +209,49 @@
             device_id_type=MESH_ID,
         )
 
-    def send_on(page, chunk):
-        @pl.when((page <= z) & (z < n - 1))
+    def goes_right(page, chunk):
+        goes = (page <= z) & (z < n - 1)
+        return goes & ~((z == n - 2) & (page == 0)) if chunk < CHUNKS else goes
+
+    def goes_left(page, chunk):
+        goes = (page >= z) & (z > 0)
+        return goes & ~((z == 1) & (page == n - 1)) if chunk < CHUNKS else goes
+
+    def send_on(page, chunk, own=False):
+        @pl.when(goes_right(page, chunk))
         def _():
-            hop(page, chunk, z + 1, right_sem).start()
-
-        @pl.when((page >= z) & (z > 0))
+            hop(page, chunk, z + 1, right_sem, own).start()
+
+        @pl.when(goes_left(page, chunk))
         def _():
-            hop(page, chunk, z - 1, left_sem).start()
-
-    loads[0].wait()
-    for chunk in range(CHUNKS):
-        send_on(z, chunk)
-    loads[1].wait()
-    send_on(z, CHUNKS)
-
+            hop(page, chunk, z - 1, left_sem, own).start()
+
+    for chunk in (CHUNKS, *range(CHUNKS)):
+        send_on(z, chunk, own=True)
+
+    def pack_copy(k, to):
+        ref = (pack, pack_slot)[k]
+        return pltpu.make_async_remote_copy(
+            src_ref=ref,
+            dst_ref=ref,
+            send_sem=pack_send_sem.at[k],
+            recv_sem=pack_recv_sem.at[k],
+            device_id={"page": to},
+            device_id_type=MESH_ID,
+        )
+
+    def pack_return(to):
+        return pltpu.make_async_remote_copy(
+            src_ref=pack_send,
+            dst_ref=pack_back,
+            send_sem=pack_send_sem.at[2],
+            recv_sem=pack_recv_sem.at[2],
+            device_id={"page": to},
+            device_id_type=MESH_ID,
+        )
+
+    loads[4].wait()
+    loads[5].wait()
     slot_row = jnp.zeros(index_ref.shape, jnp.float32)
     for a in range(adapters):
         slot_row = jnp.where(index_ref[...] == a, slot_ref[a].astype(jnp.float32), slot_row)
@@ -213,6 +259,41 @@
     lane = lax.broadcasted_iota(jnp.int32, (rows, 128), 1)
     half = (lane // rank).astype(jnp.float32)
     loads[2].wait()
+    cap = pack.shape[0]
+
+    @pl.when(end)
+    def _():
+        lowest = (opposite * group).astype(jnp.float32)
+        mine = (slot_row >= lowest) & (slot_row < lowest + float(group))
+        marks = jnp.broadcast_to(jnp.where(mine, 1.0, 0.0), (16, rows)).astype(jnp.bfloat16)
+        earlier = lax.broadcasted_iota(jnp.int32, (rows, rows), 0) < lax.broadcasted_iota(
+            jnp.int32, (rows, rows), 1
+        )
+        position = jnp.dot(
+            marks,
+            jnp.where(earlier, 1.0, 0.0).astype(jnp.bfloat16),
+            preferred_element_type=jnp.float32,
+        )[:1]
+        target = jnp.where(mine, position, -1.0)
+        spots = lax.broadcasted_iota(jnp.int32, (cap, rows), 0).astype(jnp.float32)
+        place[...] = jnp.where(spots == target, 1.0, 0.0).astype(jnp.bfloat16)
+
+        @pl.loop(0, depth // 512)
+        def _(b):
+            columns = pl.ds(pl.multiple_of(b * 512, 512), 512)
+            pack[:, columns] = jnp.dot(
+                place[...], tok[:, columns], preferred_element_type=jnp.float32
+            ).astype(jnp.bfloat16)
+
+        pack_slot[...] = lax.dot_general(
+            jnp.broadcast_to(slot_row, (16, rows)).astype(jnp.bfloat16),
+            place[...],
+            (((1,), (1,)), ((), ())),
+            preferred_element_type=jnp.float32,
+        )[: pack_slot.shape[0]]
+        for k in range(2):
+            pack_copy(k, helper).start()
+
     loads[3].wait()
     blocks, width = part.shape[0], part.shape[2]
 
@@ -242,38 +323,73 @@
     for k in range(2):
         to_sibling(k).start()
 
-    def pick(page, product):
+    def pick(page, product, slot, half):
         first = (page * group).astype(jnp.float32) + half
-        total = jnp.zeros((rows, 128), jnp.float32)
+        total = jnp.zeros(slot.shape, jnp.float32)
         for g in range(group * rank // 128):
             hit = slot == first + float(g * (128 // rank))
             total += jnp.where(hit, product[:, g * 128 : g * 128 + 128], 0.0)
         return total
 
-    for turn in range(n):
-        page = page_in_turn(z, turn, n)
+    def product_of(ref, page, chunk):
+        return jnp.dot(
+            ref[:, chunk * piece : chunk * piece + piece],
+            down_all[page, pl.ds(chunk * piece, piece), :],
+            preferred_element_type=jnp.float32,
+        )
+
+    def take_page(page, arrives):
         for chunk in range(CHUNKS):
-            if turn:
+            if arrives:
                 hop(page, chunk, z, left_sem).wait_recv()
                 send_on(page, chunk)
-            span = pl.ds(chunk * piece, piece)
-            product = jnp.dot(
-                tok[:, chunk * piece : chunk * piece + piece],
-                down_all[page, span, :],
-                preferred_element_type=jnp.float32,
-            )
-            if turn == 0 and chunk == 0:
-                picked[...] = pick(page, product)
-            else:
-                picked[...] += pick(page, product)
-        if turn:
-            hop(page, CHUNKS, z, left_sem).wait_recv()
-            send_on(page, CHUNKS)
-        if turn == 0:
-            for k in range(2):
-                to_sibling(k).wait_recv()
-            part[2 * (1 - t) + s] += near_base[1 - t]
-            base_far.start()
+            picked[...] += pick(page, product_of(tok, page, chunk), slot, half)
+
+    loads[0].wait()
+    loads[1].wait()
+    picked[...] = jnp.zeros_like(picked)
+    take_page(z, False)
+    for k in range(2):
+        to_sibling(k).wait_recv()
+    part[2 * (1 - t) + s] += near_base[1 - t]
+    base_far.start()
+    for turn in range(1, n - 1):
+        page = page_in_turn(z, turn, n)
+        hop(page, CHUNKS, z, left_sem).wait_recv()
+        send_on(page, CHUNKS)
+        take_page(page, True)
+
+    last = page_in_turn(z, n - 1, n)
+    hop(last, CHUNKS, z, left_sem).wait_recv()
+    send_on(last, CHUNKS)
+
+    @pl.when(~end)
+    def _():
+        for k in range(2):
+            pack_copy(k, z).wait_recv()
+        their_slot = jnp.transpose(jnp.broadcast_to(pack_slot[:1], (128, cap)))
+        theirs = jnp.zeros((cap, 128), jnp.float32)
+        for chunk in range(CHUNKS):
+            hop(last, chunk, z, left_sem).wait_recv()
+            send_on(last, chunk)
+            theirs += pick(last, product_of(pack, last, chunk), their_slot, half[:cap])
+        theirs += pltpu.roll(theirs, rank, 1)
+        pack_send[...] = jnp.where(
+            lane[: cap // 2] < rank, theirs[: cap // 2], theirs[cap // 2 :]
+        ).astype(jnp.bfloat16)
+        pack_return(helped).start()
+        for chunk in range(CHUNKS):
+            picked[...] += pick(last, product_of(tok, last, chunk), slot, half)
+
+    @pl.when(end)
+    def _():
+        pack_return(z).wait_recv()
+        back = pack_back[...].astype(jnp.float32)
+        back = jnp.concatenate([back, pltpu.roll(back, rank, 1)], axis=0)
+        back = jnp.where(lane[:cap] < rank, back, 0.0).astype(jnp.bfloat16)
+        picked[...] += lax.dot_general(
+            place[...], back, (((0,), (0,)), ((), ())), preferred_element_type=jnp.float32
+        )
 
     folded = picked[...] + pltpu.roll(picked[...], rank, 1)
     low = lane[: rows // 2] < rank
@@ -288,7 +404,8 @@
     )
     near.start()
     near.wait_recv()
-    far_send[...] = shrink_send[...] + near_shrink[...]
+    chip_sum = shrink_send[...] + near_shrink[...]
+    far_send[...] = chip_sum.astype(jnp.bfloat16)
     far = pltpu.make_async_remote_copy(
         src_ref=far_send,
         dst_ref=far_shrink,
@@ -301,7 +418,7 @@
     base_far.wait_recv()
     part[2 * t + s] += near_base[t] + far_base[...]
     far.wait_recv()
-    both = far_send[...] + far_shrink[...]
+    both = chip_sum + far_shrink[...].astype(jnp.float32)
     both = both.astype(jnp.bfloat16).astype(jnp.float32)
     turned = pltpu.roll(both, rank, 1)
     shrink = jnp.concatenate(
@@ -327,17 +444,27 @@
     base_far.wait_send()
     near.wait_send()
     far.wait_send()
+
+    @pl.when(end)
+    def _():
+        for k in range(2):
+            pack_copy(k, helper).wait_send()
+
+    @pl.when(~end)
+    def _():
+        pack_return(helped).wait_send()
+
     for turn in range(n):
         page = page_in_turn(z, turn, n)
         for chunk in range(CHUNKS + 1):
 
-            @pl.when((page <= z) & (z < n - 1))
+            @pl.when(goes_right(page, chunk))
             def _():
-                hop(page, chunk, z + 1, right_sem).wait_send()
-
-            @pl.when((page >= z) & (z > 0))
+                hop(page, chunk, z + 1, right_sem, turn == 0).wait_send()
+
+            @pl.when(goes_left(page, chunk))
             def _():
-                hop(page, chunk, z - 1, left_sem).wait_send()
+                hop(page, chunk, z - 1, left_sem, turn == 0).wait_send()
 
 
 def gather_weights_body(
@@ -354,38 +481,44 @@
     share = adapter_up_weight.shape[1]
     blocks = base_value_weight.shape[1] // share
     adapters = adapter_storage_slot.shape[0]
+    cap = rows // 2
     f32, bf16 = jnp.float32, jnp.bfloat16
     return pl.pallas_call(
         functools.partial(gather_kernel, n, adapters),
         out_shape=jax.ShapeDtypeStruct((rows, share), bf16),
-        in_specs=[pl.BlockSpec(memory_space=pl.ANY)] * 4
-        + [
-            pl.BlockSpec(memory_space=pltpu.VMEM),
-            pl.BlockSpec(memory_space=pltpu.SMEM),
-        ],
+        in_specs=[pl.BlockSpec(memory_space=pltpu.HBM)] * 6,
         out_specs=pl.BlockSpec(memory_space=pltpu.VMEM),
         scratch_shapes=[
+            pltpu.VMEM((1, rows), jnp.int32),
+            pltpu.SMEM((adapters,), jnp.int32),
             pltpu.VMEM((rows, depth), bf16),
             pltpu.VMEM(base_value_weight.shape, bf16),
             pltpu.VMEM((n, depth, width), bf16),
             pltpu.VMEM((n, width, share), bf16),
+            pltpu.VMEM((cap, depth), bf16),
+            pltpu.VMEM((8, cap), f32),
+            pltpu.VMEM((cap, rows), bf16),
+            pltpu.VMEM((cap // 2, 128), bf16),
+            pltpu.VMEM((cap // 2, 128), bf16),
             pltpu.VMEM((blocks, rows, share), f32),
             pltpu.VMEM((rows, 128), f32),
             pltpu.VMEM((2, rows, share), f32),
             pltpu.VMEM((rows, share), f32),
             pltpu.VMEM((rows // 2, 128), f32),
             pltpu.VMEM((rows // 2, 128), f32),
-            pltpu.VMEM((rows // 2, 128), f32),
-            pltpu.VMEM((rows // 2, 128), f32),
-            pltpu.SemaphoreType.DMA((4,)),
+            pltpu.VMEM((rows // 2, 128), bf16),
+            pltpu.VMEM((rows // 2, 128), bf16),
+            pltpu.SemaphoreType.DMA((6,)),
             pltpu.SemaphoreType.DMA((n, CHUNKS + 1)),
             pltpu.SemaphoreType.DMA((n, CHUNKS + 1)),
             pltpu.SemaphoreType.DMA((n, CHUNKS + 1)),
+            pltpu.SemaphoreType.DMA((3,)),
+            pltpu.SemaphoreType.DMA((3,)),
             pltpu.SemaphoreType.DMA((5,)),
             pltpu.SemaphoreType.DMA((5,)),
         ],
         compiler_params=pltpu.CompilerParams(
-            collective_id=0, has_side_effects=True, vmem_limit_bytes=48 * 1024 * 1024
+            collective_id=0, has_side_effects=True, vmem_limit_bytes=60 * 1024 * 1024
         ),
     )(
         tokens,
@@ -399,7 +532,7 @@
 
 def solution(mesh):
     sizes = mesh.shape
-    gathers = sizes["page"] <= 4 and sizes["tp"] == 2 and sizes["sub"] == 2
+    gathers = sizes["page"] == 4 and sizes["tp"] == 2 and sizes["sub"] == 2
     return jax.shard_map(
         gather_weights_body if gathers else exchange_rows_body,
         mesh=mesh,

time: 94.7 us -> 68.6 us (0.72)
  Pallas kernels: 88.6 us -> 66.7 us
  local copies, waits for them, and re-layouts: 5.76 us -> 1.67 us
    pallas_call x1, Pallas kernels: 88.6 us -> 66.7 us  [gather_weights_body(): pl.pallas_call(functools.partial(gather_kernel, n, adapters), out_shape=j...]
    unnamed x11 -> x1, local copies, waits for them, and re-layouts: 5.76 us -> 1.67 us
where the time goes in v2:
time: 68.6 us; the launch traced here: 68.4 us
  Pallas kernels  66.7 us (97%)
  local copies, waits for them, and re-layouts  1.67 us (2%)
    pallas_call x1, Pallas kernels, gather_weights_body(): pl.pallas_call(functools.partial(gather_kernel, n, adapters), out_shape=j...  66.7 us
    unnamed x1, local copies, waits for them, and re-layouts  1.67 us

profile of v2, /device:TPU:0, one launch (start us, length us, event | category | flops | bytes accessed | tf_op | source)
XLA Modules:
  0.0 68.4 jit_solution(15355944117977609042)
XLA Ops:
  0.0 66.7 %shard_map.64 = bf16[512,256]{1,0:T(8,128)(2,1)} custom-call(bf16[512,2048]{1,0:T(8,128)(2,1)} %tokens_hbm.1, bf16[2048,1024]{1,0:T(8,128)(2,1)} %base_hbm.1, bf16[2048,256]{1,0:T(8,128)(2,1)} %down_hbm.1, bf16[256,256]{1,0:T(8,128)(2,1)} %up_hbm.1, s32[1,512]{1,0:T(1,128)} %bitcast.1, s32[16]{0:T(128)} %slot_hbm.1), custom_call_target="tpu_custom_call" | custom-call | tf_op jit(solution)/shard_map/pallas_call | solution.py:486
  66.7 1.7 %copy.8 = bf16[512,256]{1,0:T(8,128)(2,1)} copy(bf16[512,256]{1,0:T(8,128)(2,1)} %shard_map.64) | data formatting | bytes 524288

commit v3 on v2

--- a/solution.py
+++ b/solution.py
@@ -107,7 +107,7 @@
 
 
 MESH_ID = pl.DeviceIdType.MESH
-CHUNKS = 2
+CHUNKS = 4
 
 
 def page_in_turn(z, turn, n):
@@ -338,30 +338,43 @@
             preferred_element_type=jnp.float32,
         )
 
-    def take_page(page, arrives):
-        for chunk in range(CHUNKS):
-            if arrives:
-                hop(page, chunk, z, left_sem).wait_recv()
-                send_on(page, chunk)
-            picked[...] += pick(page, product_of(tok, page, chunk), slot, half)
+    def take_piece(page, chunk):
+        picked[...] += pick(page, product_of(tok, page, chunk), slot, half)
+
+    def pass_on(page, chunk):
+        hop(page, chunk, z, left_sem).wait_recv()
+        send_on(page, chunk)
 
     loads[0].wait()
     loads[1].wait()
     picked[...] = jnp.zeros_like(picked)
-    take_page(z, False)
+    for chunk in range(CHUNKS):
+        take_piece(z, chunk)
     for k in range(2):
         to_sibling(k).wait_recv()
     part[2 * (1 - t) + s] += near_base[1 - t]
     base_far.start()
-    for turn in range(1, n - 1):
-        page = page_in_turn(z, turn, n)
-        hop(page, CHUNKS, z, left_sem).wait_recv()
-        send_on(page, CHUNKS)
-        take_page(page, True)
-
     last = page_in_turn(z, n - 1, n)
-    hop(last, CHUNKS, z, left_sem).wait_recv()
-    send_on(last, CHUNKS)
+    between = [page_in_turn(z, turn, n) for turn in range(1, n - 1)]
+    for page in between:
+        pass_on(page, CHUNKS)
+
+    @pl.when(~end)
+    def _():
+        for chunk in range(CHUNKS):
+            for page in between:
+                pass_on(page, chunk)
+            for page in between:
+                take_piece(page, chunk)
+
+    @pl.when(end)
+    def _():
+        for page in between:
+            for chunk in range(CHUNKS):
+                pass_on(page, chunk)
+                take_piece(page, chunk)
+
+    pass_on(last, CHUNKS)
 
     @pl.when(~end)
     def _():
@@ -370,16 +383,16 @@
         their_slot = jnp.transpose(jnp.broadcast_to(pack_slot[:1], (128, cap)))
         theirs = jnp.zeros((cap, 128), jnp.float32)
         for chunk in range(CHUNKS):
-            hop(last, chunk, z, left_sem).wait_recv()
-            send_on(last, chunk)
+            pass_on(last, chunk)
             theirs += pick(last, product_of(pack, last, chunk), their_slot, half[:cap])
+            if chunk < CHUNKS - 1:
+                take_piece(last, chunk)
         theirs += pltpu.roll(theirs, rank, 1)
         pack_send[...] = jnp.where(
             lane[: cap // 2] < rank, theirs[: cap // 2], theirs[cap // 2 :]
         ).astype(jnp.bfloat16)
         pack_return(helped).start()
-        for chunk in range(CHUNKS):
-            picked[...] += pick(last, product_of(tok, last, chunk), slot, half)
+        take_piece(last, CHUNKS - 1)
 
     @pl.when(end)
     def _():

time: 68.6 us -> 67.7 us (0.987)
  Pallas kernels: 66.7 us -> 65.9 us
    pallas_call x1, Pallas kernels: 66.7 us -> 65.9 us  [gather_weights_body(): pl.pallas_call(functools.partial(gather_kernel, n, adapters), out_shape=j...]
where the time goes in v3:
time: 67.7 us; the launch traced here: 67.6 us
  Pallas kernels  65.9 us (97%)
  local copies, waits for them, and re-layouts  1.67 us (2%)
    pallas_call x1, Pallas kernels, gather_weights_body(): pl.pallas_call(functools.partial(gather_kernel, n, adapters), out_shape=j...  65.9 us
    unnamed x1, local copies, waits for them, and re-layouts  1.67 us

profile of v3, /device:TPU:0, one launch (start us, length us, event | category | flops | bytes accessed | tf_op | source)
XLA Modules:
  0.0 67.6 jit_solution(17348642818187011833)
XLA Ops:
  0.0 65.9 %shard_map.64 = bf16[512,256]{1,0:T(8,128)(2,1)} custom-call(bf16[512,2048]{1,0:T(8,128)(2,1)} %tokens_hbm.1, bf16[2048,1024]{1,0:T(8,128)(2,1)} %base_hbm.1, bf16[2048,256]{1,0:T(8,128)(2,1)} %down_hbm.1, bf16[256,256]{1,0:T(8,128)(2,1)} %up_hbm.1, s32[1,512]{1,0:T(1,128)} %bitcast.1, s32[16]{0:T(128)} %slot_hbm.1), custom_call_target="tpu_custom_call" | custom-call | tf_op jit(solution)/shard_map/pallas_call | solution.py:499
  65.9 1.7 %copy.8 = bf16[512,256]{1,0:T(8,128)(2,1)} copy(bf16[512,256]{1,0:T(8,128)(2,1)} %shard_map.64) | data formatting | bytes 524288

commit v4 on v3

--- a/solution.py
+++ b/solution.py
@@ -107,7 +107,12 @@
 
 
 MESH_ID = pl.DeviceIdType.MESH
-CHUNKS = 4
+BOUNDS = (0, 2, 8, 12, 16)
+CHUNKS = len(BOUNDS) - 1
+
+
+def piece_of(chunk, depth):
+    return BOUNDS[chunk] * depth // 16, (BOUNDS[chunk + 1] - BOUNDS[chunk]) * depth // 16
 
 
 def page_in_turn(z, turn, n):
@@ -136,6 +141,7 @@
     down_all,
     up_all,
     pack,
+    pack_first,
     pack_slot,
     place,
     pack_send,
@@ -161,7 +167,6 @@
     rows, depth = tok.shape
     rank = ADAPTER_RANK
     group = down_all.shape[2] // rank
-    piece = depth // CHUNKS
 
     loads = [
         pltpu.make_async_copy(down_hbm, down_all.at[z], load_sem.at[0]),
@@ -192,11 +197,13 @@
     helped = jnp.where(z == 1, 0, n - 1)
     helper = jnp.where(z == 0, 1, n - 2)
     opposite = n - 1 - z
+    second = jnp.where(z == 0, n - 2, 1)
 
     def hop(page, chunk, to, sems, own=False):
         if chunk < CHUNKS:
-            ref = down_all.at[page, pl.ds(chunk * piece, piece), :]
-            src = down_hbm.at[pl.ds(chunk * piece, piece), :] if own else ref
+            span = pl.ds(*piece_of(chunk, depth))
+            ref = down_all.at[page, span, :]
+            src = down_hbm.at[span, :] if own else ref
         else:
             ref = up_all.at[page]
             src = up_hbm if own else ref
@@ -211,10 +218,14 @@
 
     def goes_right(page, chunk):
         goes = (page <= z) & (z < n - 1)
+        if chunk == 0:
+            return goes & ~((z == n - 2) & (page <= 1))
         return goes & ~((z == n - 2) & (page == 0)) if chunk < CHUNKS else goes
 
     def goes_left(page, chunk):
         goes = (page >= z) & (z > 0)
+        if chunk == 0:
+            return goes & ~((z == 1) & (page >= n - 2))
         return goes & ~((z == 1) & (page == n - 1)) if chunk < CHUNKS else goes
 
     def send_on(page, chunk, own=False):
@@ -230,7 +241,7 @@
         send_on(z, chunk, own=True)
 
     def pack_copy(k, to):
-        ref = (pack, pack_slot)[k]
+        ref = (pack, pack_slot.at[0], pack_first, pack_slot.at[1])[k]
         return pltpu.make_async_remote_copy(
             src_ref=ref,
             dst_ref=ref,
@@ -240,12 +251,12 @@
             device_id_type=MESH_ID,
         )
 
-    def pack_return(to):
+    def pack_return(k, to):
         return pltpu.make_async_remote_copy(
-            src_ref=pack_send,
-            dst_ref=pack_back,
-            send_sem=pack_send_sem.at[2],
-            recv_sem=pack_recv_sem.at[2],
+            src_ref=pack_send.at[k],
+            dst_ref=pack_back.at[k],
+            send_sem=pack_send_sem.at[4 + k],
+            recv_sem=pack_recv_sem.at[4 + k],
             device_id={"page": to},
             device_id_type=MESH_ID,
         )
@@ -263,36 +274,41 @@
 
     @pl.when(end)
     def _():
-        lowest = (opposite * group).astype(jnp.float32)
-        mine = (slot_row >= lowest) & (slot_row < lowest + float(group))
-        marks = jnp.broadcast_to(jnp.where(mine, 1.0, 0.0), (16, rows)).astype(jnp.bfloat16)
         earlier = lax.broadcasted_iota(jnp.int32, (rows, rows), 0) < lax.broadcasted_iota(
             jnp.int32, (rows, rows), 1
         )
-        position = jnp.dot(
-            marks,
-            jnp.where(earlier, 1.0, 0.0).astype(jnp.bfloat16),
-            preferred_element_type=jnp.float32,
-        )[:1]
-        target = jnp.where(mine, position, -1.0)
+        earlier = jnp.where(earlier, 1.0, 0.0).astype(jnp.bfloat16)
         spots = lax.broadcasted_iota(jnp.int32, (cap, rows), 0).astype(jnp.float32)
-        place[...] = jnp.where(spots == target, 1.0, 0.0).astype(jnp.bfloat16)
-
-        @pl.loop(0, depth // 512)
-        def _(b):
-            columns = pl.ds(pl.multiple_of(b * 512, 512), 512)
-            pack[:, columns] = jnp.dot(
-                place[...], tok[:, columns], preferred_element_type=jnp.float32
-            ).astype(jnp.bfloat16)
-
-        pack_slot[...] = lax.dot_general(
-            jnp.broadcast_to(slot_row, (16, rows)).astype(jnp.bfloat16),
-            place[...],
-            (((1,), (1,)), ((), ())),
-            preferred_element_type=jnp.float32,
-        )[: pack_slot.shape[0]]
-        for k in range(2):
-            pack_copy(k, helper).start()
+        for k, page in ((1, second), (0, opposite)):
+            lowest = (page * group).astype(jnp.float32)
+            mine = (slot_row >= lowest) & (slot_row < lowest + float(group))
+            marks = jnp.broadcast_to(jnp.where(mine, 1.0, 0.0), (16, rows)).astype(jnp.bfloat16)
+            position = jnp.dot(marks, earlier, preferred_element_type=jnp.float32)[:1]
+            target = jnp.where(mine, position, -1.0)
+            place[k] = jnp.where(spots == target, 1.0, 0.0).astype(jnp.bfloat16)
+            if k:
+                pack_first[...] = jnp.dot(
+                    place[k],
+                    tok[:, pl.ds(*piece_of(0, depth))],
+                    preferred_element_type=jnp.float32,
+                ).astype(jnp.bfloat16)
+            else:
+
+                @pl.loop(0, depth // 512)
+                def _(b):
+                    columns = pl.ds(pl.multiple_of(b * 512, 512), 512)
+                    pack[:, columns] = jnp.dot(
+                        place[0], tok[:, columns], preferred_element_type=jnp.float32
+                    ).astype(jnp.bfloat16)
+
+            pack_slot[k] = lax.dot_general(
+                jnp.broadcast_to(slot_row, (16, rows)).astype(jnp.bfloat16),
+                place[k],
+                (((1,), (1,)), ((), ())),
+                preferred_element_type=jnp.float32,
+            )[: pack_slot.shape[1]]
+            for c in range(2 * k, 2 * k + 2):
+                pack_copy(c, helper).start()
 
     loads[3].wait()
     blocks, width = part.shape[0], part.shape[2]
@@ -333,8 +349,8 @@
 
     def product_of(ref, page, chunk):
         return jnp.dot(
-            ref[:, chunk * piece : chunk * piece + piece],
-            down_all[page, pl.ds(chunk * piece, piece), :],
+            ref[:, pl.ds(*piece_of(chunk, depth))],
+            down_all[page, pl.ds(*piece_of(chunk, depth)), :],
             preferred_element_type=jnp.float32,
         )
 
@@ -359,6 +375,27 @@
     for page in between:
         pass_on(page, CHUNKS)
 
+    def return_pack(k, theirs):
+        theirs += pltpu.roll(theirs, rank, 1)
+        pack_send[k] = jnp.where(
+            lane[: cap // 2] < rank, theirs[: cap // 2], theirs[cap // 2 :]
+        ).astype(jnp.bfloat16)
+        pack_return(k, helped).start()
+
+    def slot_of_pack(k):
+        pack_copy(2 * k, z).wait_recv()
+        pack_copy(2 * k + 1, z).wait_recv()
+        return jnp.transpose(jnp.broadcast_to(pack_slot[k, :1], (128, cap)))
+
+    def place_back(k):
+        pack_return(k, z).wait_recv()
+        back = pack_back[k].astype(jnp.float32)
+        back = jnp.concatenate([back, pltpu.roll(back, rank, 1)], axis=0)
+        back = jnp.where(lane[:cap] < rank, back, 0.0).astype(jnp.bfloat16)
+        picked[...] += lax.dot_general(
+            place[k], back, (((0,), (0,)), ((), ())), preferred_element_type=jnp.float32
+        )
+
     @pl.when(~end)
     def _():
         for chunk in range(CHUNKS):
@@ -366,43 +403,33 @@
                 pass_on(page, chunk)
             for page in between:
                 take_piece(page, chunk)
-
-    @pl.when(end)
-    def _():
-        for page in between:
-            for chunk in range(CHUNKS):
-                pass_on(page, chunk)
-                take_piece(page, chunk)
-
-    pass_on(last, CHUNKS)
-
-    @pl.when(~end)
-    def _():
-        for k in range(2):
-            pack_copy(k, z).wait_recv()
-        their_slot = jnp.transpose(jnp.broadcast_to(pack_slot[:1], (128, cap)))
+        pass_on(last, CHUNKS)
+        first_slot = slot_of_pack(1)
+        product = jnp.dot(
+            pack_first[...],
+            down_all[opposite, pl.ds(*piece_of(0, depth)), :],
+            preferred_element_type=jnp.float32,
+        )
+        return_pack(1, pick(opposite, product, first_slot, half[:cap]))
+        their_slot = slot_of_pack(0)
         theirs = jnp.zeros((cap, 128), jnp.float32)
         for chunk in range(CHUNKS):
             pass_on(last, chunk)
             theirs += pick(last, product_of(pack, last, chunk), their_slot, half[:cap])
             if chunk < CHUNKS - 1:
                 take_piece(last, chunk)
-        theirs += pltpu.roll(theirs, rank, 1)
-        pack_send[...] = jnp.where(
-            lane[: cap // 2] < rank, theirs[: cap // 2], theirs[cap // 2 :]
-        ).astype(jnp.bfloat16)
-        pack_return(helped).start()
+        return_pack(0, theirs)
         take_piece(last, CHUNKS - 1)
 
     @pl.when(end)
     def _():
-        pack_return(z).wait_recv()
-        back = pack_back[...].astype(jnp.float32)
-        back = jnp.concatenate([back, pltpu.roll(back, rank, 1)], axis=0)
-        back = jnp.where(lane[:cap] < rank, back, 0.0).astype(jnp.bfloat16)
-        picked[...] += lax.dot_general(
-            place[...], back, (((0,), (0,)), ((), ())), preferred_element_type=jnp.float32
-        )
+        for turn, page in enumerate(between):
+            for chunk in range(turn, CHUNKS):
+                pass_on(page, chunk)
+                take_piece(page, chunk)
+        place_back(1)
+        pass_on(last, CHUNKS)
+        place_back(0)
 
     folded = picked[...] + pltpu.roll(picked[...], rank, 1)
     low = lane[: rows // 2] < rank
@@ -460,12 +487,13 @@
 
     @pl.when(end)
     def _():
+        for k in range(4):
+            pack_copy(k, helper).wait_send()
+
+    @pl.when(~end)
+    def _():
         for k in range(2):
-            pack_copy(k, helper).wait_send()
-
-    @pl.when(~end)
-    def _():
-        pack_return(helped).wait_send()
+            pack_return(k, helped).wait_send()
 
     for turn in range(n):
         page = page_in_turn(z, turn, n)
@@ -509,10 +537,11 @@
             pltpu.VMEM((n, depth, width), bf16),
             pltpu.VMEM((n, width, share), bf16),
             pltpu.VMEM((cap, depth), bf16),
-            pltpu.VMEM((8, cap), f32),
-            pltpu.VMEM((cap, rows), bf16),
-            pltpu.VMEM((cap // 2, 128), bf16),
-            pltpu.VMEM((cap // 2, 128), bf16),
+            pltpu.VMEM((cap, piece_of(0, depth)[1]), bf16),
+            pltpu.VMEM((2, 8, cap), f32),
+            pltpu.VMEM((2, cap, rows), bf16),
+            pltpu.VMEM((2, cap // 2, 128), bf16),
+            pltpu.VMEM((2, cap // 2, 128), bf16),
             pltpu.VMEM((blocks, rows, share), f32),
             pltpu.VMEM((rows, 128), f32),
             pltpu.VMEM((2, rows, share), f32),
@@ -525,8 +554,8 @@
             pltpu.SemaphoreType.DMA((n, CHUNKS + 1)),
             pltpu.SemaphoreType.DMA((n, CHUNKS + 1)),
             pltpu.SemaphoreType.DMA((n, CHUNKS + 1)),
-            pltpu.SemaphoreType.DMA((3,)),
-            pltpu.SemaphoreType.DMA((3,)),
+            pltpu.SemaphoreType.DMA((6,)),
+            pltpu.SemaphoreType.DMA((6,)),
             pltpu.SemaphoreType.DMA((5,)),
             pltpu.SemaphoreType.DMA((5,)),
         ],

time: 67.7 us -> 68.6 us (1.013)
  Pallas kernels: 65.9 us -> 66.8 us
    pallas_call x1, Pallas kernels: 65.9 us -> 66.8 us  [gather_weights_body(): pl.pallas_call(functools.partial(gather_kernel, n, adapters), out_shape=j...]
where the time goes in v4:
time: 68.6 us; the launch traced here: 68.5 us
  Pallas kernels  66.8 us (97%)
  local copies, waits for them, and re-layouts  1.67 us (2%)
    pallas_call x1, Pallas kernels, gather_weights_body(): pl.pallas_call(functools.partial(gather_kernel, n, adapters), out_shape=j...  66.8 us
    unnamed x1, local copies, waits for them, and re-layouts  1.67 us

profile of v4, /device:TPU:0, one launch (start us, length us, event | category | flops | bytes accessed | tf_op | source)
XLA Modules:
  0.0 68.5 jit_solution(2955507189580166411)
XLA Ops:
  0.0 66.8 %shard_map.64 = bf16[512,256]{1,0:T(8,128)(2,1)} custom-call(bf16[512,2048]{1,0:T(8,128)(2,1)} %tokens_hbm.1, bf16[2048,1024]{1,0:T(8,128)(2,1)} %base_hbm.1, bf16[2048,256]{1,0:T(8,128)(2,1)} %down_hbm.1, bf16[256,256]{1,0:T(8,128)(2,1)} %up_hbm.1, s32[1,512]{1,0:T(1,128)} %bitcast.1, s32[16]{0:T(128)} %slot_hbm.1), custom_call_target="tpu_custom_call" | custom-call | tf_op jit(solution)/shard_map/pallas_call | solution.py:527
  66.8 1.7 %copy.8 = bf16[512,256]{1,0:T(8,128)(2,1)} copy(bf16[512,256]{1,0:T(8,128)(2,1)} %shard_map.64) | data formatting | bytes 524288

commit v5 on v3

--- a/solution.py
+++ b/solution.py
@@ -107,7 +107,12 @@
 
 
 MESH_ID = pl.DeviceIdType.MESH
-CHUNKS = 4
+BOUNDS = (0, 4, 9, 14, 16)
+CHUNKS = len(BOUNDS) - 1
+
+
+def piece_of(chunk, depth):
+    return BOUNDS[chunk] * depth // 16, (BOUNDS[chunk + 1] - BOUNDS[chunk]) * depth // 16
 
 
 def page_in_turn(z, turn, n):
@@ -161,7 +166,6 @@
     rows, depth = tok.shape
     rank = ADAPTER_RANK
     group = down_all.shape[2] // rank
-    piece = depth // CHUNKS
 
     loads = [
         pltpu.make_async_copy(down_hbm, down_all.at[z], load_sem.at[0]),
@@ -192,11 +196,13 @@
     helped = jnp.where(z == 1, 0, n - 1)
     helper = jnp.where(z == 0, 1, n - 2)
     opposite = n - 1 - z
+    outer = jnp.where(z == 1, 0, n - 1)
 
     def hop(page, chunk, to, sems, own=False):
         if chunk < CHUNKS:
-            ref = down_all.at[page, pl.ds(chunk * piece, piece), :]
-            src = down_hbm.at[pl.ds(chunk * piece, piece), :] if own else ref
+            span = pl.ds(*piece_of(chunk, depth))
+            ref = down_all.at[page, span, :]
+            src = down_hbm.at[span, :] if own else ref
         else:
             ref = up_all.at[page]
             src = up_hbm if own else ref
@@ -218,11 +224,13 @@
         return goes & ~((z == 1) & (page == n - 1)) if chunk < CHUNKS else goes
 
     def send_on(page, chunk, own=False):
-        @pl.when(goes_right(page, chunk))
+        late = own and chunk == CHUNKS - 1
+
+        @pl.when(goes_right(page, chunk) & ~((z == 1) & late))
         def _():
             hop(page, chunk, z + 1, right_sem, own).start()
 
-        @pl.when(goes_left(page, chunk))
+        @pl.when(goes_left(page, chunk) & ~((z == n - 2) & late))
         def _():
             hop(page, chunk, z - 1, left_sem, own).start()
 
@@ -333,8 +341,8 @@
 
     def product_of(ref, page, chunk):
         return jnp.dot(
-            ref[:, chunk * piece : chunk * piece + piece],
-            down_all[page, pl.ds(chunk * piece, piece), :],
+            ref[:, pl.ds(*piece_of(chunk, depth))],
+            down_all[page, pl.ds(*piece_of(chunk, depth)), :],
             preferred_element_type=jnp.float32,
         )
 
@@ -361,11 +369,22 @@
 
     @pl.when(~end)
     def _():
-        for chunk in range(CHUNKS):
-            for page in between:
-                pass_on(page, chunk)
-            for page in between:
-                take_piece(page, chunk)
+        for chunk in range(CHUNKS - 1):
+            pass_on(outer, chunk)
+            pass_on(opposite, chunk)
+            take_piece(outer, chunk)
+            take_piece(opposite, chunk)
+        pass_on(outer, CHUNKS - 1)
+
+        @pl.when(z == 1)
+        def _():
+            hop(z, CHUNKS - 1, z + 1, right_sem, True).start()
+
+        @pl.when(z == n - 2)
+        def _():
+            hop(z, CHUNKS - 1, z - 1, left_sem, True).start()
+
+        take_piece(outer, CHUNKS - 1)
 
     @pl.when(end)
     def _():
@@ -392,7 +411,9 @@
             lane[: cap // 2] < rank, theirs[: cap // 2], theirs[cap // 2 :]
         ).astype(jnp.bfloat16)
         pack_return(helped).start()
+        pass_on(opposite, CHUNKS - 1)
         take_piece(last, CHUNKS - 1)
+        take_piece(opposite, CHUNKS - 1)
 
     @pl.when(end)
     def _():

time: 67.7 us -> 68.8 us (1.016)
  Pallas kernels: 65.9 us -> 67 us
    pallas_call x1, Pallas kernels: 65.9 us -> 67 us  [gather_weights_body(): pl.pallas_call(functools.partial(gather_kernel, n, adapters), out_shape=j...]
where the time goes in v5:
time: 68.8 us; the launch traced here: 68.6 us
  Pallas kernels  67 us (97%)
  local copies, waits for them, and re-layouts  1.67 us (2%)
    pallas_call x1, Pallas kernels, gather_weights_body(): pl.pallas_call(functools.partial(gather_kernel, n, adapters), out_shape=j...  67 us
    unnamed x1, local copies, waits for them, and re-layouts  1.67 us

profile of v5, /device:TPU:0, one launch (start us, length us, event | category | flops | bytes accessed | tf_op | source)
XLA Modules:
  0.0 68.6 jit_solution(143722437112315144)
XLA Ops:
  0.0 67.0 %shard_map.64 = bf16[512,256]{1,0:T(8,128)(2,1)} custom-call(bf16[512,2048]{1,0:T(8,128)(2,1)} %tokens_hbm.1, bf16[2048,1024]{1,0:T(8,128)(2,1)} %base_hbm.1, bf16[2048,256]{1,0:T(8,128)(2,1)} %down_hbm.1, bf16[256,256]{1,0:T(8,128)(2,1)} %up_hbm.1, s32[1,512]{1,0:T(1,128)} %bitcast.1, s32[16]{0:T(128)} %slot_hbm.1), custom_call_target="tpu_custom_call" | custom-call | tf_op jit(solution)/shard_map/pallas_call | solution.py:520
  67.0 1.7 %copy.8 = bf16[512,256]{1,0:T(8,128)(2,1)} copy(bf16[512,256]{1,0:T(8,128)(2,1)} %shard_map.64) | data formatting | bytes 524288

commit v6 on v3

--- a/solution.py
+++ b/solution.py
@@ -128,7 +128,8 @@
     up_hbm,
     index_hbm,
     slot_hbm,
-    out_ref,
+    lora_ref,
+    base_out,
     index_ref,
     slot_ref,
     tok,
@@ -430,6 +431,8 @@
     far.start()
     base_far.wait_recv()
     part[2 * t + s] += near_base[t] + far_base[...]
+    store = pltpu.make_async_copy(part.at[2 * t + s], base_out, load_sem.at[6])
+    store.start()
     far.wait_recv()
     both = chip_sum + far_shrink[...].astype(jnp.float32)
     both = both.astype(jnp.bfloat16).astype(jnp.float32)
@@ -449,8 +452,8 @@
         up_all[...].reshape(n * group * rank, up_all.shape[2]),
         preferred_element_type=jnp.float32,
     )
-    lora = (expand * adapter_scale).astype(jnp.bfloat16).astype(jnp.float32)
-    out_ref[...] = (part[2 * t + s] + lora).astype(jnp.bfloat16)
+    lora_ref[...] = (expand * adapter_scale).astype(jnp.bfloat16)
+    store.wait()
 
     for k in range(2):
         to_sibling(k).wait_send()
@@ -496,11 +499,17 @@
     adapters = adapter_storage_slot.shape[0]
     cap = rows // 2
     f32, bf16 = jnp.float32, jnp.bfloat16
-    return pl.pallas_call(
+    lora, base = pl.pallas_call(
         functools.partial(gather_kernel, n, adapters),
-        out_shape=jax.ShapeDtypeStruct((rows, share), bf16),
+        out_shape=(
+            jax.ShapeDtypeStruct((rows, share), bf16),
+            jax.ShapeDtypeStruct((rows, share), f32),
+        ),
         in_specs=[pl.BlockSpec(memory_space=pltpu.HBM)] * 6,
-        out_specs=pl.BlockSpec(memory_space=pltpu.VMEM),
+        out_specs=(
+            pl.BlockSpec(memory_space=pltpu.VMEM),
+            pl.BlockSpec(memory_space=pltpu.HBM),
+        ),
         scratch_shapes=[
             pltpu.VMEM((1, rows), jnp.int32),
             pltpu.SMEM((adapters,), jnp.int32),
@@ -521,7 +530,7 @@
             pltpu.VMEM((rows // 2, 128), f32),
             pltpu.VMEM((rows // 2, 128), bf16),
             pltpu.VMEM((rows // 2, 128), bf16),
-            pltpu.SemaphoreType.DMA((6,)),
+            pltpu.SemaphoreType.DMA((7,)),
             pltpu.SemaphoreType.DMA((n, CHUNKS + 1)),
             pltpu.SemaphoreType.DMA((n, CHUNKS + 1)),
             pltpu.SemaphoreType.DMA((n, CHUNKS + 1)),
@@ -541,6 +550,7 @@
         row_adapter_index.reshape(1, rows),
         adapter_storage_slot,
     )
+    return (base + lora.astype(f32)).astype(bf16)
 
 
 def solution(mesh):

time: 67.7 us -> 67.9 us (level)
  other arithmetic: 0 us -> 1.87 us
  local copies, waits for them, and re-layouts: 1.67 us -> 0 us
    convert_element_type x0 -> x1, other arithmetic: none -> 1.87 us  [gather_weights_body(): return (base + lora.astype(f32)).astype(bf16)]
    unnamed x1 -> x0, local copies, waits for them, and re-layouts: 1.67 us -> none
where the time goes in v6:
time: 67.9 us; the launch traced here: 67.8 us
  Pallas kernels  65.9 us (97%)
  other arithmetic  1.87 us (3%)
    pallas_call x1, Pallas kernels, gather_weights_body(): pl.pallas_call(functools.partial(gather_kernel, n, adapters), out_shape=(...  65.9 us
    convert_element_type x1, other arithmetic, gather_weights_body(): return (base + lora.astype(f32)).astype(bf16)  1.87 us

profile of v6, /device:TPU:0, one launch (start us, length us, event | category | flops | bytes accessed | tf_op | source)
XLA Modules:
  0.0 67.8 jit_solution(8093953139912960683)
XLA Ops:
  0.0 65.9 %shard_map.64 = (bf16[512,256]{1,0:T(8,128)(2,1)}, f32[512,256]{1,0:T(8,128)}) custom-call(bf16[512,2048]{1,0:T(8,128)(2,1)} %tokens_hbm.1, bf16[2048,1024]{1,0:T(8,128)(2,1)} %base_hbm.1, bf16[2048,256]{1,0:T(8,128)(2,1)} %down_hbm.1, bf16[256,256]{1,0:T(8,128)(2,1)} %up_hbm.1, s32[1,512]{1,0:T(1,128)} %bitcast.1, s32[16]{0:T(128)} %slot_hbm.1), custom_call_target="tpu_custom_call" | custom-call | tf_op jit(solution)/shard_map/pallas_call | solution.py:502
  65.9 1.9 %add_convert_fusion = bf16[512,256]{1,0:T(8,128)(2,1)} fusion(f32[512,256]{1,0:T(8,128)} %get-tuple-element.7, bf16[512,256]{1,0:T(8,128)(2,1)} %get-tuple-element.8), kind=kLoop, calls=%fused_computation | loop fusion | flops 393216 | bytes 1048576 | tf_op jit(solution)/shard_map/convert_element_type | solution.py:553
